TPU v7x, 128 devices: a whole 4x4x4 slice. The times are simulated.
128 devices in a mesh: seq: 8 (over z, y_hi), grp: 16 (over y_lo, x, core).
Axes of the slice: x: 4, y: 4 (y_hi: 2, y_lo: 2; y = y_hi * 2 + y_lo), z: 4, core: 2. Of those that a mesh axis runs over, the one named last changes fastest.
Arguments:
- self_query: bfloat16 [16, 1024, 5120], P('grp', 'seq'), may hold values from -250 to 250
- self_key: bfloat16 [16, 1024, 5120], P('grp', 'seq'), may hold values from -12 to 12
- self_value: bfloat16 [16, 1024, 5120], P('grp', 'seq'), may hold values from -6 to 6
- self_upstream: bfloat16 [16, 1024, 5120], P('grp', 'seq'), may hold values from -6 to 6
- cross_query: bfloat16 [16, 1024, 5120], P('grp', 'seq'), may hold values from -250 to 250
- context_key: bfloat16 [512, 5120], replicated, may hold values from -12 to 12
- context_value: bfloat16 [512, 5120], replicated, may hold values from -6 to 6
- cross_upstream: bfloat16 [16, 1024, 5120], P('grp', 'seq'), may hold values from -6 to 6
Outputs:
- query_grad: bfloat16 [16, 1024, 5120], P('grp', 'seq')
- key_grad: bfloat16 [16, 1024, 5120], P('grp', 'seq')
- value_grad: bfloat16 [16, 1024, 5120], P('grp', 'seq')
- cross_query_grad: bfloat16 [16, 1024, 5120], P('grp', 'seq')
- context_key_grad: float32 [512, 5120], P(None, 'seq')
- context_value_grad: float32 [512, 5120], P(None, 'seq')
All inputs are finite; a program needn't handle non-finite values.
Results may differ from a plain program's by a relative error of at most 0.013.
Values may be sent and summed in bfloat16 or wider, within the bound.
A program may use at most 256 MiB of HBM per device.

v0:
```python
import jax
import jax.numpy as jnp
from jax import lax
from jax.sharding import PartitionSpec as P

HD = 128


def pick_rows(row_count, largest):
    block_rows = min(largest, row_count)
    while row_count % block_rows:
        block_rows = block_rows - 1
    return block_rows


def block_backward(queries, key_in, value_in, upstream):
    row_count, head_count, head_depth = queries.shape
    block_rows = pick_rows(row_count, 512)
    block_count = row_count // block_rows
    piece_rows = pick_rows(block_rows, 128)
    piece_count = block_rows // piece_rows
    scaling = HD ** (-0.5)

    def advance(totals, pieces):
        query_block, upstream_block = pieces
        scores = (
            jnp.einsum("nhe,mhe->hnm", query_block, key_in, preferred_element_type=jnp.float32)
            * scaling
        )
        weights = jax.nn.softmax(scores, axis=-1)
        rounded = weights.astype(jnp.bfloat16)
        output = jnp.einsum("hnm,mhe->nhe", rounded, value_in, preferred_element_type=jnp.float32)
        row_inner = jnp.sum(upstream_block.astype(jnp.float32) * output, axis=-1)
        grad_prob = jnp.einsum(
            "nhe,mhe->hnm", upstream_block, value_in, preferred_element_type=jnp.float32
        )
        grad_score = (
            weights * (grad_prob - jnp.transpose(row_inner)[:, :, None]) * scaling
        ).astype(jnp.bfloat16)
        query_grad = jnp.einsum(
            "hnm,mhe->nhe", grad_score, key_in, preferred_element_type=jnp.float32
        ).astype(jnp.bfloat16)
        score_split = grad_score.reshape(head_count, piece_count, piece_rows, grad_score.shape[2])
        weight_split = rounded.reshape(head_count, piece_count, piece_rows, rounded.shape[2])
        query_split = query_block.reshape(piece_count, piece_rows, head_count, head_depth)
        upstream_split = upstream_block.reshape(piece_count, piece_rows, head_count, head_depth)
        key_terms = jnp.einsum(
            "hgnm,gnhe->gmhe", score_split, query_split, preferred_element_type=jnp.float32
        )
        value_terms = jnp.einsum(
            "hgnm,gnhe->gmhe", weight_split, upstream_split, preferred_element_type=jnp.float32
        )
        key_sum = totals[0] + jnp.sum(key_terms, axis=0)
        value_sum = totals[1] + jnp.sum(value_terms, axis=0)
        return ((key_sum, value_sum), query_grad)

    zero_sum = jnp.zeros(key_in.shape, jnp.float32)
    blocked = (
        queries.reshape(block_count, block_rows, head_count, head_depth),
        upstream.reshape(block_count, block_rows, head_count, head_depth),
    )
    running, query_grads = lax.scan(advance, (zero_sum, zero_sum), blocked)
    return (query_grads.reshape(row_count, head_count, head_depth), running[0], running[1])


def shards(
    self_query,
    self_key,
    self_value,
    self_upstream,
    cross_query,
    context_key,
    context_value,
    cross_upstream,
):
    token_count = self_query.shape[1]
    full_width = self_query.shape[2]
    head_count = full_width // HD
    text_rows = context_key.shape[0]
    seq_count = lax.axis_size("seq")
    group_heads = head_count // seq_count

    def to_heads(tensor):
        return tensor.reshape(token_count, head_count, HD)

    def to_groups(tensor):
        return tensor.reshape(token_count, seq_count, group_heads, HD)

    pieces = (
        lax.all_to_all(to_groups(self_query[0]), "seq", split_axis=1, concat_axis=0, tiled=True),
        lax.all_to_all(to_groups(self_key[0]), "seq", split_axis=1, concat_axis=0, tiled=True),
        lax.all_to_all(to_groups(self_value[0]), "seq", split_axis=1, concat_axis=0, tiled=True),
        lax.all_to_all(to_groups(self_upstream[0]), "seq", split_axis=1, concat_axis=0, tiled=True),
    )
    rows = pieces[0].shape[0]
    items = pieces[0].shape[2]

    def flat(tensor):
        return tensor.reshape(rows, items, HD)

    query_part, key_part, value_part = block_backward(
        flat(pieces[0]), flat(pieces[1]), flat(pieces[2]), flat(pieces[3])
    )
    shape_back = (rows, 1, items, HD)
    query_grad, key_grad, value_grad = (
        lax.all_to_all(
            query_part.reshape(shape_back), "seq", split_axis=0, concat_axis=1, tiled=True
        ),
        lax.all_to_all(
            key_part.astype(jnp.bfloat16).reshape(shape_back),
            "seq",
            split_axis=0,
            concat_axis=1,
            tiled=True,
        ),
        lax.all_to_all(
            value_part.astype(jnp.bfloat16).reshape(shape_back),
            "seq",
            split_axis=0,
            concat_axis=1,
            tiled=True,
        ),
    )
    columns = full_width // seq_count
    offset = lax.axis_index("seq") * columns
    context_heads = context_key.reshape(text_rows, head_count, HD)
    value_heads = context_value.reshape(text_rows, head_count, HD)
    cross_grad, context_keys_part, context_values_part = block_backward(
        to_heads(cross_query[0]), context_heads, value_heads, to_heads(cross_upstream[0])
    )
    key_partial = context_keys_part.reshape(text_rows, full_width)
    value_partial = context_values_part.reshape(text_rows, full_width)
    key_whole, value_whole = lax.psum((key_partial, value_partial), ("seq", "grp"))
    key_total = lax.dynamic_slice_in_dim(key_whole, offset, columns, 1)
    value_total = lax.dynamic_slice_in_dim(value_whole, offset, columns, 1)
    shape_out = (1, token_count, full_width)
    return (
        query_grad.reshape(shape_out),
        key_grad.reshape(shape_out),
        value_grad.reshape(shape_out),
        cross_grad.reshape(shape_out),
        key_total,
        value_total,
    )


def solution(mesh):
    return jax.shard_map(
        shards,
        mesh=mesh,
        in_specs=(
            P("grp", "seq", None),
            P("grp", "seq", None),
            P("grp", "seq", None),
            P("grp", "seq", None),
            P("grp", "seq", None),
            P(),
            P(),
            P("grp", "seq", None),
        ),
        out_specs=(
            P("grp", "seq", None),
            P("grp", "seq", None),
            P("grp", "seq", None),
            P("grp", "seq", None),
            P(None, "seq"),
            P(None, "seq"),
        ),
        check_vma=False,
    )
```

profile of v0, /device:TPU:1, one launch (start us, length us, event | category | flops | bytes accessed | tf_op | source)
XLA Modules:
  0.0 414.7 jit_solution(14000686213218465211)
XLA Ops:
  9.7 8.5 %all-to-all-start = ((bf16[128,8,5,128]{0,3,2,1:T(8,128)(2,1)}), bf16[128,8,5,128]{0,3,2,1:T(8,128)(2,1)S(1)}, u32[]{:S(2)}, u32[]{:S(2)}) async-start(bf16[128,8,5,128]{0,3,2,1:T(8,128)(2,1)} %bitcast), calls=%async_computation | async-start | bytes 2621440 | tf_op jit(solution)/shard_map/all_to_all | solution.py:90
  21.4 7.9 %copy.145 = bf16[512,5120]{0,1:T(8,128)(2,1)} copy(bf16[512,5120]{1,0:T(8,128)(2,1)} %param.15) | data formatting | bytes 10485760 | tf_op jit(solution)/shard_map/reshape | solution.py:126
  29.3 10.0 %fusion.36 = (f32[40,128]{1,0:T(8,128)S(1)}, f32[40,128,512]{2,1,0:T(8,128)}) fusion(bf16[128,40,128]{0,2,1:T(8,128)(2,1)S(1)} %bitcast.198, bf16[512,40,128]{0,2,1:T(8,128)(2,1)} %bitcast.196), kind=kOutput, calls=%fused_computation.42 | convolution fusion | flops 678953472 | bytes 17059840 | tf_op jit(solution)/shard_map/while/body/eval_jaxpr/sub | solution.py:30
  39.3 6.6 %all-to-all-start.1 = ((bf16[128,8,5,128]{0,3,2,1:T(8,128)(2,1)}), bf16[128,8,5,128]{0,3,2,1:T(8,128)(2,1)}, u32[]{:S(2)}, u32[]{:S(2)}) async-start(bf16[128,8,5,128]{0,3,2,1:T(8,128)(2,1)} %bitcast.211), calls=%async_computation.1 | async-start | bytes 2621440 | tf_op jit(solution)/shard_map/all_to_all | solution.py:91
  46.0 7.3 %fusion.26 = bf16[40,128,512]{2,1,0:T(8,128)(2,1)} fusion(f32[40,128,512]{2,1,0:T(8,128)} %get-tuple-element.175, f32[40,128]{1,0:T(8,128)S(1)} %get-tuple-element.174), kind=kLoop, calls=%fused_computation.31 | loop fusion | flops 5242880 | bytes 15749120 | tf_op jit(solution)/shard_map/while/body/eval_jaxpr/convert_element_type | solution.py:31
  59.9 8.0 %copy.146 = bf16[512,5120]{0,1:T(8,128)(2,1)} copy(bf16[512,5120]{1,0:T(8,128)(2,1)} %param.16) | data formatting | bytes 10485760 | tf_op jit(solution)/shard_map/reshape | solution.py:127
  73.4 6.7 %all-to-all-start.2 = ((bf16[128,8,5,128]{0,3,2,1:T(8,128)(2,1)}), bf16[128,8,5,128]{0,3,2,1:T(8,128)(2,1)}, u32[]{:S(2)}, u32[]{:S(2)}) async-start(bf16[128,8,5,128]{0,3,2,1:T(8,128)(2,1)} %bitcast.212), calls=%async_computation.2 | async-start | bytes 2621440 | tf_op jit(solution)/shard_map/all_to_all | solution.py:93
  80.1 8.3 %multiply_convert_fusion.1 = bf16[40,128,512]{2,1,0:T(8,128)(2,1)} fusion(f32[40,128]{1,0:T(8,128)S(1)} %bitcast.223, f32[40,128,512]{2,1,0:T(8,128)} %get-tuple-element.175, f32[40,128]{1,0:T(8,128)S(1)} %get-tuple-element.174, bf16[128,40,128]{0,2,1:T(8,128)(2,1)S(1)} %bitcast.203, bf16[512,40,128]{0,2,1:T(8,128)(2,1)} %bitcast.208), kind=kOutput, calls=%fused_computation.25 | convolution fusion | flops 684195840 | bytes 22323200 | tf_op jit(solution)/shard_map/while/body/eval_jaxpr/nhe,mhe->hnm/dot_general | solution.py:34
  88.4 9.4 %all-to-all-done.2 = bf16[128,8,5,128]{0,3,2,1:T(8,128)(2,1)} async-done(((bf16[128,8,5,128]{0,3,2,1:T(8,128)(2,1)}), bf16[128,8,5,128]{0,3,2,1:T(8,128)(2,1)}, u32[]{:S(2)}, u32[]{:S(2)}) %all-to-all-start.2) | async-done | bytes 1310752 | tf_op jit(solution)/shard_map/all_to_all | solution.py:93
  102.6 7.8 %fusion.37 = f32[40,512,128]{1,2,0:T(8,128)} fusion(bf16[128,40,128]{0,2,1:T(8,128)(2,1)S(1)} %bitcast.199, bf16[40,128,512]{2,1,0:T(8,128)(2,1)} %multiply_convert_fusion.1), kind=kOutput, calls=%fused_computation.43 | convolution fusion | flops 671088640 | bytes 17039360 | tf_op jit(solution)/shard_map/while/body/eval_jaxpr/hgnm,gnhe->gmhe/dot_general | solution.py:47
  110.4 11.5 %copy.127 = f32[512,5120]{1,0:T(8,128)} copy(f32[512,5120]{0,1:T(8,128)} %bitcast.193) | data formatting | bytes 20971520 | tf_op jit(solution)/shard_map/reshape | solution.py:131
  121.9 8.0 %fusion.38 = f32[40,512,128]{1,2,0:T(8,128)} fusion(bf16[128,40,128]{0,2,1:T(8,128)(2,1)S(1)} %bitcast.204, bf16[40,128,512]{2,1,0:T(8,128)(2,1)} %fusion.26), kind=kOutput, calls=%fused_computation.44 | convolution fusion | flops 671088640 | bytes 17039360 | tf_op jit(solution)/shard_map/while/body/eval_jaxpr/hgnm,gnhe->gmhe/dot_general | solution.py:50
  129.8 11.5 %copy.128 = f32[512,5120]{1,0:T(8,128)} copy(f32[512,5120]{0,1:T(8,128)} %bitcast.192) | data formatting | bytes 20971520 | tf_op jit(solution)/shard_map/reshape | solution.py:132
  152.1 76.3 %while.3 = (s32[]{:T(128)}, f32[1024,5,128]{0,2,1:T(8,128)}, f32[1024,5,128]{0,2,1:T(8,128)}, bf16[2,512,5,128]{3,1,0,2:T(8,128)(2,1)}, bf16[2,512,5,128]{3,1,0,...) while((s32[]{:T(128)}, f32[1024,5,128]{0,2,1:T(8,128)}, ...), condition=%wide.region_4.0_spmd.clone, body=%wide.region_0.4_spmd.clone.sunk | while | flops 4056676864 | bytes 158648704 | solution.py:62
  153.5 8.6 %fusion.92 = (f32[5,512]{1,0:T(8,128)S(1)}, f32[5,512,1024]{2,1,0:T(8,128)}) fusion(bf16[1024,5,128]{2,0,1:T(8,128)(2,1)} %get-tuple-element.260, bf16[1,512,5,128]{3,1,0,2:T(8,128)(2,1)S(1)} %get-tuple-element.231), kind=kOutput, calls=%fused_computation.41.clone.1 | convolution fusion | flops 678953984 | bytes 12462080 | tf_op jit(solution)/shard_map/while/body/eval_jaxpr/sub | solution.py:30
  170.3 7.0 %multiply_convert_fusion.3 = bf16[5,512,1024]{2,1,0:T(8,128)(2,1)} fusion(f32[5,512]{1,0:T(8,128)S(1)} %bitcast.224, f32[5,512,1024]{2,1,0:T(8,128)} %get-tuple-element.232, f32[5,512]{1,0:T(8,128)S(1)} %get-tuple-element.233, bf16[1024,5,128]{0,2,1:T(8,128)(2,1)S(1)} %copy-done.7, bf16[1,512,5,128]{3,1,0,2:T(8,128)(2,1)S(1)} %get-tuple-element.234), kind=kOutput, calls=%fused_computation.1.clone.1 | convolution fusion | flops 684195840 | bytes 17715200 | tf_op jit(solution)/shard_map/while/body/eval_jaxpr/nhe,mhe->hnm/dot_general | solution.py:34
  190.7 8.5 %fusion.92 = (f32[5,512]{1,0:T(8,128)S(1)}, f32[5,512,1024]{2,1,0:T(8,128)}) fusion(bf16[1024,5,128]{2,0,1:T(8,128)(2,1)} %get-tuple-element.260, bf16[1,512,5,128]{3,1,0,2:T(8,128)(2,1)S(1)} %get-tuple-element.231), kind=kOutput, calls=%fused_computation.41.clone.1 | convolution fusion | flops 678953984 | bytes 12462080 | tf_op jit(solution)/shard_map/while/body/eval_jaxpr/sub | solution.py:30
  207.4 7.2 %multiply_convert_fusion.3 = bf16[5,512,1024]{2,1,0:T(8,128)(2,1)} fusion(f32[5,512]{1,0:T(8,128)S(1)} %bitcast.224, f32[5,512,1024]{2,1,0:T(8,128)} %get-tuple-element.232, f32[5,512]{1,0:T(8,128)S(1)} %get-tuple-element.233, bf16[1024,5,128]{0,2,1:T(8,128)(2,1)S(1)} %copy-done.7, bf16[1,512,5,128]{3,1,0,2:T(8,128)(2,1)S(1)} %get-tuple-element.234), kind=kOutput, calls=%fused_computation.1.clone.1 | convolution fusion | flops 684195840 | bytes 17715200 | tf_op jit(solution)/shard_map/while/body/eval_jaxpr/nhe,mhe->hnm/dot_general | solution.py:34
  214.6 6.2 %bitcast_add_fusion.4 = f32[1024,5,128]{0,2,1:T(8,128)} fusion(f32[1024,5,128]{0,2,1:T(8,128)} %get-tuple-element.246, bf16[4,128,5,128]{3,1,0,2:T(8,128)(2,1)S(1)} %bitcast.195, bf16[5,4,128,1024]{3,2,1,0:T(8,128)(2,1)} %bitcast.189, pred[]{:T(512)S(6)} %compare.3), kind=kOutput, calls=%fused_computation.9.clone.1 | convolution fusion | flops 672399360 | bytes 11141121 | tf_op jit(solution)/shard_map/while/body/eval_jaxpr/hgnm,gnhe->gmhe/dot_general | solution.py:47
  232.0 6.9 %all-to-all-start.4 = ((bf16[1024,1,5,128]{3,2,1,0:T(8,128)(2,1)}), bf16[1024,1,5,128]{3,2,1,0:T(8,128)(2,1)}, u32[]{:S(2)}, u32[]{:S(2)}) async-start(bf16[1024,1,5,128]{3,2,1,0:T(8,128)(2,1)} %copy.110), calls=%async_computation.4 | async-start | bytes 4194304 | tf_op jit(solution)/shard_map/all_to_all | solution.py:106
  242.0 23.9 %all-to-all-done.4 = bf16[1024,1,5,128]{3,2,1,0:T(8,128)(2,1)} async-done(((bf16[1024,1,5,128]{3,2,1,0:T(8,128)(2,1)}), bf16[1024,1,5,128]{3,2,1,0:T(8,128)(2,1)}, u32[]{:S(2)}, u32[]{:S(2)}) %all-to-all-start.4) | async-done | bytes 1310752 | tf_op jit(solution)/shard_map/all_to_all | solution.py:106
  274.5 24.0 %all-to-all-done.5 = bf16[1024,1,5,128]{3,2,1,0:T(8,128)(2,1)} async-done(((bf16[1024,1,5,128]{3,2,1,0:T(8,128)(2,1)}), bf16[1024,1,5,128]{3,2,1,0:T(8,128)(2,1)}, u32[]{:S(2)}, u32[]{:S(2)}) %all-to-all-start.5) | async-done | bytes 1310752 | tf_op jit(solution)/shard_map/all_to_all | solution.py:109
  322.5 14.6 %all-to-all-done.6 = bf16[1024,1,5,128]{3,2,1,0:T(8,128)(2,1)S(1)} async-done(((bf16[1024,1,5,128]{3,2,1,0:T(8,128)(2,1)}), bf16[1024,1,5,128]{3,2,1,0:T(8,128)(2,1)S(1)}, u32[]{:S(2)}, u32[]{:S(2)}) %all-to-all-start.6) | async-done | bytes 1310752 | tf_op jit(solution)/shard_map/all_to_all | solution.py:116
  339.5 65.0 %all-reduce.3.cloned.1.call-done = (f32[512,5120]{1,0:T(8,128)}, f32[512,5120]{1,0:T(8,128)}) async-done(((f32[512,5120]{1,0:T(8,128)}, f32[512,5120]{1,0:T(8,128)}), (f32[512,5120]{1,0:T(8,128)}, f32[512,5120]{1,0:T(8,128)})) %all-reduce.3.cloned.1.call-update) | async-done | bytes 20971536 | tf_op jit(solution)/shard_map/psum | solution.py:133
  (99 shorter events, 117.1 us)
Async XLA Ops:
  7.2 11.0 %copy-start.5 = (bf16[1,128,5120]{2,1,0:T(8,128)(2,1)S(1)}, bf16[1,128,5120]{2,1,0:T(8,128)(2,1)}, u32[]{:S(2)}) copy-start(bf16[1,128,5120]{2,1,0:T(8,128)(2,1)} %param.11) | copy-start | bytes 3932164
  9.7 29.6 %all-to-all-start = ((bf16[128,8,5,128]{0,3,2,1:T(8,128)(2,1)}), bf16[128,8,5,128]{0,3,2,1:T(8,128)(2,1)S(1)}, u32[]{:S(2)}, u32[]{:S(2)}) async-start(bf16[128,8,5,128]{0,3,2,1:T(8,128)(2,1)} %bitcast), calls=%async_computation | async-start | bytes 2621440 | tf_op jit(solution)/shard_map/all_to_all | solution.py:90
  39.3 13.9 %copy-start.3 = (bf16[128,8,5,128]{0,3,2,1:T(8,128)(2,1)}, bf16[128,8,5,128]{0,3,2,1:T(8,128)(2,1)S(1)}, u32[]{:S(2)}) copy-start(bf16[128,8,5,128]{0,3,2,1:T(8,128)(2,1)S(1)} %all-to-all-done) | copy-start | bytes 3932164
  39.3 34.1 %all-to-all-start.1 = ((bf16[128,8,5,128]{0,3,2,1:T(8,128)(2,1)}), bf16[128,8,5,128]{0,3,2,1:T(8,128)(2,1)}, u32[]{:S(2)}, u32[]{:S(2)}) async-start(bf16[128,8,5,128]{0,3,2,1:T(8,128)(2,1)} %bitcast.211), calls=%async_computation.1 | async-start | bytes 2621440 | tf_op jit(solution)/shard_map/all_to_all | solution.py:91
  73.4 24.4 %all-to-all-start.2 = ((bf16[128,8,5,128]{0,3,2,1:T(8,128)(2,1)}), bf16[128,8,5,128]{0,3,2,1:T(8,128)(2,1)}, u32[]{:S(2)}, u32[]{:S(2)}) async-start(bf16[128,8,5,128]{0,3,2,1:T(8,128)(2,1)} %bitcast.212), calls=%async_computation.2 | async-start | bytes 2621440 | tf_op jit(solution)/shard_map/all_to_all | solution.py:93
  97.9 51.0 %all-to-all-start.3 = ((bf16[128,8,5,128]{0,3,2,1:T(8,128)(2,1)}), bf16[128,8,5,128]{0,3,2,1:T(8,128)(2,1)}, u32[]{:S(2)}, u32[]{:S(2)}) async-start(bf16[128,8,5,128]{0,3,2,1:T(8,128)(2,1)} %bitcast.210), calls=%async_computation.3 | async-start | bytes 2621440 | tf_op jit(solution)/shard_map/all_to_all | solution.py:92
  102.4 302.1 %all-reduce.3.cloned.1.call-start = ((), (), s32[]{:S(2)}) async-start(), calls=%async_computation.7 | async-start | bytes 41943040 | tf_op jit(solution)/shard_map/psum | solution.py:133
  162.1 5.8 %copy-start.7 = (bf16[1024,5,128]{0,2,1:T(8,128)(2,1)S(1)}, bf16[1024,5,128]{0,2,1:T(8,128)(2,1)}, u32[]{:S(2)}) copy-start(bf16[1024,5,128]{0,2,1:T(8,128)(2,1)} %get-tuple-element.262) | copy-start | bytes 3932164 | tf_op jit(solution)/shard_map/while
  177.3 5.3 %slice-start = ((s8[5242880]{0:T(1024)(128)(4,1)}), s8[1048576]{0:T(1024)(128)(4,1)S(1)}, s32[]{:S(2)}) async-start(s8[5242880]{0:T(1024)(128)(4,1)} %bitcast.186), calls=%async_computation.8 | async-start | bytes 2097152 | tf_op jit(solution)/shard_map/while
  177.3 5.3 %slice-start.1 = ((s8[5242880]{0:T(1024)(128)(4,1)}), s8[4194304]{0:T(1024)(128)(4,1)S(1)}, s32[]{:S(2)}) async-start(s8[5242880]{0:T(1024)(128)(4,1)} %bitcast.186), calls=%async_computation.9 | async-start | bytes 8388608 | tf_op jit(solution)/shard_map/while
  177.3 7.9 %slice-start.2 = ((s8[5242880]{0:T(1024)(128)(4,1)}), s8[4194304]{0:T(1024)(128)(4,1)S(1)}, s32[]{:S(2)}) async-start(s8[5242880]{0:T(1024)(128)(4,1)} %bitcast.190), calls=%async_computation.10 | async-start | bytes 8388608 | tf_op jit(solution)/shard_map/while
  182.7 3.8 copy-start.8
  199.2 5.8 %copy-start.7 = (bf16[1024,5,128]{0,2,1:T(8,128)(2,1)S(1)}, bf16[1024,5,128]{0,2,1:T(8,128)(2,1)}, u32[]{:S(2)}) copy-start(bf16[1024,5,128]{0,2,1:T(8,128)(2,1)} %get-tuple-element.262) | copy-start | bytes 3932164 | tf_op jit(solution)/shard_map/while
  214.6 6.2 %slice-start = ((s8[5242880]{0:T(1024)(128)(4,1)}), s8[1048576]{0:T(1024)(128)(4,1)S(1)}, s32[]{:S(2)}) async-start(s8[5242880]{0:T(1024)(128)(4,1)} %bitcast.186), calls=%async_computation.8 | async-start | bytes 2097152 | tf_op jit(solution)/shard_map/while
  214.6 6.2 %slice-start.1 = ((s8[5242880]{0:T(1024)(128)(4,1)}), s8[4194304]{0:T(1024)(128)(4,1)S(1)}, s32[]{:S(2)}) async-start(s8[5242880]{0:T(1024)(128)(4,1)} %bitcast.186), calls=%async_computation.9 | async-start | bytes 8388608 | tf_op jit(solution)/shard_map/while
  214.6 11.0 %slice-start.2 = ((s8[5242880]{0:T(1024)(128)(4,1)}), s8[4194304]{0:T(1024)(128)(4,1)S(1)}, s32[]{:S(2)}) async-start(s8[5242880]{0:T(1024)(128)(4,1)} %bitcast.190), calls=%async_computation.10 | async-start | bytes 8388608 | tf_op jit(solution)/shard_map/while
  220.7 4.8 %slice-start.3 = ((s8[5242880]{0:T(1024)(128)(4,1)}), s8[1048576]{0:T(1024)(128)(4,1)S(1)}, s32[]{:S(2)}) async-start(s8[5242880]{0:T(1024)(128)(4,1)} %bitcast.190), calls=%async_computation.11 | async-start | bytes 2097152 | tf_op jit(solution)/shard_map/while
  220.8 4.8 %copy-start.6 = (bf16[1024,5,128]{2,0,1:T(8,128)(2,1)S(1)}, bf16[1024,5,128]{2,0,1:T(8,128)(2,1)}, u32[]{:S(2)}) copy-start(bf16[1024,5,128]{2,0,1:T(8,128)(2,1)} %get-tuple-element.260) | copy-start | bytes 3932164 | tf_op jit(solution)/shard_map/while
  220.8 4.8 %copy-start.8 = (bf16[2,512,5,128]{3,1,0,2:T(8,128)(2,1)S(1)}, bf16[2,512,5,128]{3,1,0,2:T(8,128)(2,1)}, u32[]{:S(2)}) copy-start(bf16[2,512,5,128]{3,1,0,2:T(8,128)(2,1)} %get-tuple-element.248) | copy-start | bytes 3932164 | tf_op jit(solution)/shard_map/while
  232.0 6.9 %copy-start.1 = (f32[1024,5,128]{0,2,1:T(8,128)S(1)}, f32[1024,5,128]{0,2,1:T(8,128)}, u32[]{:S(2)}) copy-start(f32[1024,5,128]{0,2,1:T(8,128)} %get-tuple-element.75) | copy-start | bytes 7864324
  232.0 33.9 %all-to-all-start.4 = ((bf16[1024,1,5,128]{3,2,1,0:T(8,128)(2,1)}), bf16[1024,1,5,128]{3,2,1,0:T(8,128)(2,1)}, u32[]{:S(2)}, u32[]{:S(2)}) async-start(bf16[1024,1,5,128]{3,2,1,0:T(8,128)(2,1)} %copy.110), calls=%async_computation.4 | async-start | bytes 4194304 | tf_op jit(solution)/shard_map/all_to_all | solution.py:106
  242.0 29.4 %copy-start.2 = (f32[1024,5,128]{0,2,1:T(8,128)S(1)}, f32[1024,5,128]{0,2,1:T(8,128)}, u32[]{:S(2)}) copy-start(f32[1024,5,128]{0,2,1:T(8,128)} %get-tuple-element.76) | copy-start | bytes 7864324
  265.9 32.7 %all-to-all-start.5 = ((bf16[1024,1,5,128]{3,2,1,0:T(8,128)(2,1)}), bf16[1024,1,5,128]{3,2,1,0:T(8,128)(2,1)}, u32[]{:S(2)}, u32[]{:S(2)}) async-start(bf16[1024,1,5,128]{3,2,1,0:T(8,128)(2,1)} %bitcast.206), calls=%async_computation.5 | async-start | bytes 4194304 | tf_op jit(solution)/shard_map/all_to_all | solution.py:109
  298.5 38.5 %all-to-all-start.6 = ((bf16[1024,1,5,128]{3,2,1,0:T(8,128)(2,1)}), bf16[1024,1,5,128]{3,2,1,0:T(8,128)(2,1)S(1)}, u32[]{:S(2)}, u32[]{:S(2)}) async-start(bf16[1024,1,5,128]{3,2,1,0:T(8,128)(2,1)} %bitcast.205), calls=%async_computation.6 | async-start | bytes 4194304 | tf_op jit(solution)/shard_map/all_to_all | solution.py:116
  (7 other events, 13.3 us)
Sparse Core Ops, SparseCore 0:
  141.5 262.9 all-reduce.2
where the time goes:
time: 416 us; the launch traced here: 415 us
  waiting for transfers between devices  137 us (33%)
  matrix products  102 us (25%)
  local copies, waits for them, and re-layouts  97.9 us (24%)
  starting transfers between devices  44.4 us (11%)
  other arithmetic  18.9 us (5%)
  between operations  14.2 us (3%)
    psum x1, waiting for transfers between devices, shards(): lax.psum((key_partial, value_partial), ('seq', 'grp'))  65 us
    sub x3, matrix products, advance(): weights = jax.nn.softmax(scores, axis=-1)  27.1 us
    all_to_all x1, waiting for transfers between devices, shards(): lax.all_to_all(key_part.astype(jnp.bfloat16).reshape(shape_back), 'seq',...  24 us
    all_to_all x1, waiting for transfers between devices, shards(): lax.all_to_all(query_part.reshape(shape_back), 'seq', split_axis=0, conca...  23.9 us
    dot_general x3, matrix products, advance(): jnp.einsum('nhe,mhe->hnm', upstream_block, value_in, preferred_element_ty...  22.5 us
    unnamed x20, local copies, waits for them, and re-layouts  21 us
    dot_general x3, matrix products, advance(): jnp.einsum('hgnm,gnhe->gmhe', score_split, query_split, preferred_element...  19.3 us
    convert_element_type x3, other arithmetic, advance(): rounded = weights.astype(jnp.bfloat16)  18.9 us
  transfers between devices with their start and end apart: 8, of which 5 were waited for; matrix products, arithmetic and copies ran while one was open for 50% of the time, Pallas kernels for 0%

commit v1 on v0

--- a/solution.py
+++ b/solution.py
@@ -130,7 +130,9 @@
     )
     key_partial = context_keys_part.reshape(text_rows, full_width)
     value_partial = context_values_part.reshape(text_rows, full_width)
-    key_whole, value_whole = lax.psum((key_partial, value_partial), ("seq", "grp"))
+    key_whole, value_whole = lax.psum(
+        lax.psum((key_partial, value_partial), axis_name="grp"), axis_name="seq"
+    )
     key_total = lax.dynamic_slice_in_dim(key_whole, offset, columns, 1)
     value_total = lax.dynamic_slice_in_dim(value_whole, offset, columns, 1)
     shape_out = (1, token_count, full_width)

time: 416 us -> 1280 us (3.08)
  waiting for transfers between devices: 137 us -> 1030 us
    psum x1 -> x2, waiting for transfers between devices: 65 us -> 794 us  [the longest x1 554 us: shards(): lax.psum(lax.psum((key_partial, value_partial), axis_name='grp'), axis_na...]
    all_to_all x1, waiting for transfers between devices: 0.01 us -> 29.7 us  [shards(): lax.all_to_all(to_groups(self_key[0]), 'seq', split_axis=1, concat_axis=0...]
    all_to_all x1, waiting for transfers between devices: 0.01 us -> 27.9 us  [shards(): lax.all_to_all(to_groups(self_query[0]), 'seq', split_axis=1, concat_axis...]
    all_to_all x1, waiting for transfers between devices: 0.01 us -> 26.6 us  [shards(): lax.all_to_all(to_groups(self_value[0]), 'seq', split_axis=1, concat_axis...]
    all_to_all x1, waiting for transfers between devices: 23.9 us -> 45.1 us  [shards(): lax.all_to_all(query_part.reshape(shape_back), 'seq', split_axis=0, conca...]
    all_to_all x1, waiting for transfers between devices: 24 us -> 44.7 us  [shards(): lax.all_to_all(key_part.astype(jnp.bfloat16).reshape(shape_back), 'seq',...]
    all_to_all x1, waiting for transfers between devices: 9.43 us -> 29.6 us  [shards(): lax.all_to_all(to_groups(self_upstream[0]), 'seq', split_axis=1, concat_a...]
    all_to_all x1, waiting for transfers between devices: 14.6 us -> 29.4 us  [shards(): lax.all_to_all(value_part.astype(jnp.bfloat16).reshape(shape_back), 'seq'...]
  transfers between devices with their start and end apart: 8 -> 9, of which waited for: 5 -> 9; matrix products, arithmetic and copies ran while one was open for 50% -> 9% of each run, Pallas kernels for 0% -> 0%
where the time goes in v1:
time: 1280 us; the launch traced here: 1270 us
  waiting for transfers between devices  1030 us (80%)
  local copies, waits for them, and re-layouts  94.6 us (7%)
  matrix products  90.5 us (7%)
  starting transfers between devices  31.6 us (2%)
  other arithmetic  16.4 us (1%)
  between operations  14.3 us (1%)
    psum x1, waiting for transfers between devices, shards(): lax.psum(lax.psum((key_partial, value_partial), axis_name='grp'), axis_na...  554 us
    psum x1, waiting for transfers between devices, shards(): lax.psum((key_partial, value_partial), axis_name='grp')  240 us
    all_to_all x1, waiting for transfers between devices, shards(): lax.all_to_all(query_part.reshape(shape_back), 'seq', split_axis=0, conca...  45.1 us
    all_to_all x1, waiting for transfers between devices, shards(): lax.all_to_all(key_part.astype(jnp.bfloat16).reshape(shape_back), 'seq',...  44.7 us
    all_to_all x1, waiting for transfers between devices, shards(): lax.all_to_all(to_groups(self_key[0]), 'seq', split_axis=1, concat_axis=0...  29.7 us
    all_to_all x1, waiting for transfers between devices, shards(): lax.all_to_all(to_groups(self_upstream[0]), 'seq', split_axis=1, concat_a...  29.6 us
    all_to_all x1, waiting for transfers between devices, shards(): lax.all_to_all(value_part.astype(jnp.bfloat16).reshape(shape_back), 'seq'...  29.4 us
    all_to_all x1, waiting for transfers between devices, shards(): lax.all_to_all(to_groups(self_query[0]), 'seq', split_axis=1, concat_axis...  27.9 us
  transfers between devices with their start and end apart: 9, of which 9 were waited for; matrix products, arithmetic and copies ran while one was open for 9% of the time, Pallas kernels for 0%

profile of v1, /device:TPU:1, one launch (start us, length us, event | category | flops | bytes accessed | tf_op | source)
XLA Modules:
  0.0 1274.7 jit_solution(9623007065652247539)
XLA Ops:
  10.8 7.9 copy.145
  18.7 7.9 copy.146
  26.6 9.8 fusion.36
  36.5 5.7 fusion.26
  42.1 5.5 fusion.38
  62.3 11.5 copy.127
  73.8 11.5 copy.128
  85.5 240.2 %all-reduce.5.cloned.1.call-done = (f32[512,5120]{1,0:T(8,128)}, f32[512,5120]{1,0:T(8,128)}) async-done(((f32[512,5120]{1,0:T(8,128)}, f32[512,5120]{1,0:T(8,128)}), (f32[512,5120]{1,0:T(8,128)}, f32[512,5120]{1,0:T(8,128)})) %all-reduce.5.cloned.1.call-update) | async-done | bytes 20971536 | tf_op jit(solution)/shard_map/psum | solution.py:134
  328.4 6.6 all-to-all-start
  336.4 27.9 %all-to-all-done = bf16[128,8,5,128]{0,3,2,1:T(8,128)(2,1)S(1)} async-done(((bf16[128,8,5,128]{0,3,2,1:T(8,128)(2,1)}), bf16[128,8,5,128]{0,3,2,1:T(8,128)(2,1)S(1)}, u32[]{:S(2)}, u32[]{:S(2)}) %all-to-all-start) | async-done | bytes 1310752 | tf_op jit(solution)/shard_map/all_to_all | solution.py:90
  370.3 29.7 %all-to-all-done.1 = bf16[128,8,5,128]{0,3,2,1:T(8,128)(2,1)S(1)} async-done(((bf16[128,8,5,128]{0,3,2,1:T(8,128)(2,1)}), bf16[128,8,5,128]{0,3,2,1:T(8,128)(2,1)S(1)}, u32[]{:S(2)}, u32[]{:S(2)}) %all-to-all-start.1) | async-done | bytes 1310752 | tf_op jit(solution)/shard_map/all_to_all | solution.py:91
  406.8 29.6 %all-to-all-done.2 = bf16[128,8,5,128]{0,3,2,1:T(8,128)(2,1)} async-done(((bf16[128,8,5,128]{0,3,2,1:T(8,128)(2,1)}), bf16[128,8,5,128]{0,3,2,1:T(8,128)(2,1)}, u32[]{:S(2)}, u32[]{:S(2)}) %all-to-all-start.2) | async-done | bytes 1310752 | tf_op jit(solution)/shard_map/all_to_all | solution.py:93
  446.0 26.6 %all-to-all-done.3 = bf16[128,8,5,128]{0,3,2,1:T(8,128)(2,1)} async-done(((bf16[128,8,5,128]{0,3,2,1:T(8,128)(2,1)}), bf16[128,8,5,128]{0,3,2,1:T(8,128)(2,1)}, u32[]{:S(2)}, u32[]{:S(2)}) %all-to-all-start.3) | async-done | bytes 1310752 | tf_op jit(solution)/shard_map/all_to_all | solution.py:92
  475.8 72.3 %while.3 = (s32[]{:T(128)}, f32[1024,5,128]{0,2,1:T(8,128)}, f32[1024,5,128]{0,2,1:T(8,128)}, bf16[2,512,5,128]{3,1,0,2:T(8,128)(2,1)}, bf16[2,512,5,128]{3,1,0,...) while((s32[]{:T(128)}, f32[1024,5,128]{0,2,1:T(8,128)}, ...), condition=%wide.region_4.0_spmd.clone, body=%wide.region_0.4_spmd.clone.sunk | while | flops 4056676864 | bytes 158648704 | solution.py:62
  477.2 8.4 fusion.92
  493.4 6.7 multiply_convert_fusion.3
  512.1 8.5 fusion.92
  528.3 6.7 multiply_convert_fusion.3
  534.9 6.0 bitcast_add_fusion.4
  559.5 45.1 %all-to-all-done.4 = bf16[1024,1,5,128]{3,2,1,0:T(8,128)(2,1)} async-done(((bf16[1024,1,5,128]{3,2,1,0:T(8,128)(2,1)}), bf16[1024,1,5,128]{3,2,1,0:T(8,128)(2,1)}, u32[]{:S(2)}, u32[]{:S(2)}) %all-to-all-start.4) | async-done | bytes 1310752 | tf_op jit(solution)/shard_map/all_to_all | solution.py:106
  612.1 44.7 %all-to-all-done.5 = bf16[1024,1,5,128]{3,2,1,0:T(8,128)(2,1)} async-done(((bf16[1024,1,5,128]{3,2,1,0:T(8,128)(2,1)}), bf16[1024,1,5,128]{3,2,1,0:T(8,128)(2,1)}, u32[]{:S(2)}, u32[]{:S(2)}) %all-to-all-start.5) | async-done | bytes 1310752 | tf_op jit(solution)/shard_map/all_to_all | solution.py:109
  660.4 5.6 convolution_convert_fusion.1
  678.7 29.4 %all-to-all-done.6 = bf16[1024,1,5,128]{3,2,1,0:T(8,128)(2,1)S(1)} async-done(((bf16[1024,1,5,128]{3,2,1,0:T(8,128)(2,1)}), bf16[1024,1,5,128]{3,2,1,0:T(8,128)(2,1)S(1)}, u32[]{:S(2)}, u32[]{:S(2)}) %all-to-all-start.6) | async-done | bytes 1310752 | tf_op jit(solution)/shard_map/all_to_all | solution.py:116
  710.5 554.0 %all-reduce.7.cloned.1.call-done = (f32[512,5120]{1,0:T(8,128)}, f32[512,5120]{1,0:T(8,128)}) async-done(((f32[512,5120]{1,0:T(8,128)}, f32[512,5120]{1,0:T(8,128)}), (f32[512,5120]{1,0:T(8,128)}, f32[512,5120]{1,0:T(8,128)})) %all-reduce.7.cloned.1.call-update) | async-done | bytes 20971536 | tf_op jit(solution)/shard_map/psum | solution.py:133
  (109 shorter events, 124.9 us)
Async XLA Ops:
  7.2 318.5 %all-reduce.5.cloned.1.call-start = ((), (), s32[]{:S(2)}) async-start(), calls=%async_computation.7 | async-start | bytes 41943040 | tf_op jit(solution)/shard_map/psum | solution.py:134
  36.5 15.5 %slice-start.4 = ((s8[10485760]{0:T(1024)(128)(4,1)}), s8[4194304]{0:T(1024)(128)(4,1)S(1)}, s32[]{:S(2)}) async-start(s8[10485760]{0:T(1024)(128)(4,1)} %bitcast.198), calls=%async_computation.13 | async-start | bytes 8388608
  42.1 9.8 slice-start.5
  42.1 9.8 slice-start.6
  56.8 5.5 copy-start.3
  85.3 1179.3 %all-reduce.7.cloned.1.call-start = ((), (), s32[]{:S(2)}) async-start(), calls=%async_computation.8 | async-start | bytes 41943040 | tf_op jit(solution)/shard_map/psum | solution.py:133
  327.0 8.0 copy-start.5
  328.4 35.9 %all-to-all-start = ((bf16[128,8,5,128]{0,3,2,1:T(8,128)(2,1)}), bf16[128,8,5,128]{0,3,2,1:T(8,128)(2,1)S(1)}, u32[]{:S(2)}, u32[]{:S(2)}) async-start(bf16[128,8,5,128]{0,3,2,1:T(8,128)(2,1)} %bitcast), calls=%async_computation | async-start | bytes 2621440 | tf_op jit(solution)/shard_map/all_to_all | solution.py:90
  364.3 35.7 %all-to-all-start.1 = ((bf16[128,8,5,128]{0,3,2,1:T(8,128)(2,1)}), bf16[128,8,5,128]{0,3,2,1:T(8,128)(2,1)S(1)}, u32[]{:S(2)}, u32[]{:S(2)}) async-start(bf16[128,8,5,128]{0,3,2,1:T(8,128)(2,1)} %bitcast.214), calls=%async_computation.1 | async-start | bytes 2621440 | tf_op jit(solution)/shard_map/all_to_all | solution.py:91
  400.1 36.3 %all-to-all-start.2 = ((bf16[128,8,5,128]{0,3,2,1:T(8,128)(2,1)}), bf16[128,8,5,128]{0,3,2,1:T(8,128)(2,1)}, u32[]{:S(2)}, u32[]{:S(2)}) async-start(bf16[128,8,5,128]{0,3,2,1:T(8,128)(2,1)} %bitcast.215), calls=%async_computation.2 | async-start | bytes 2621440 | tf_op jit(solution)/shard_map/all_to_all | solution.py:93
  436.4 36.2 %all-to-all-start.3 = ((bf16[128,8,5,128]{0,3,2,1:T(8,128)(2,1)}), bf16[128,8,5,128]{0,3,2,1:T(8,128)(2,1)}, u32[]{:S(2)}, u32[]{:S(2)}) async-start(bf16[128,8,5,128]{0,3,2,1:T(8,128)(2,1)} %bitcast.213), calls=%async_computation.3 | async-start | bytes 2621440 | tf_op jit(solution)/shard_map/all_to_all | solution.py:92
  485.7 5.4 copy-start.7
  500.0 5.2 slice-start
  500.0 5.2 slice-start.1
  500.0 7.7 slice-start.2
  520.5 5.4 copy-start.7
  534.9 6.0 slice-start
  534.9 6.0 slice-start.1
  534.9 10.4 slice-start.2
  551.7 4.6 copy-start.1
  551.8 52.8 %all-to-all-start.4 = ((bf16[1024,1,5,128]{3,2,1,0:T(8,128)(2,1)}), bf16[1024,1,5,128]{3,2,1,0:T(8,128)(2,1)}, u32[]{:S(2)}, u32[]{:S(2)}) async-start(bf16[1024,1,5,128]{3,2,1,0:T(8,128)(2,1)} %copy.110), calls=%async_computation.4 | async-start | bytes 4194304 | tf_op jit(solution)/shard_map/all_to_all | solution.py:106
  559.5 49.5 %copy-start.2 = (f32[1024,5,128]{0,2,1:T(8,128)S(1)}, f32[1024,5,128]{0,2,1:T(8,128)}, u32[]{:S(2)}) copy-start(f32[1024,5,128]{0,2,1:T(8,128)} %get-tuple-element.76) | copy-start | bytes 7864324
  604.5 52.2 %all-to-all-start.5 = ((bf16[1024,1,5,128]{3,2,1,0:T(8,128)(2,1)}), bf16[1024,1,5,128]{3,2,1,0:T(8,128)(2,1)}, u32[]{:S(2)}, u32[]{:S(2)}) async-start(bf16[1024,1,5,128]{3,2,1,0:T(8,128)(2,1)} %bitcast.208), calls=%async_computation.5 | async-start | bytes 4194304 | tf_op jit(solution)/shard_map/all_to_all | solution.py:109
  656.8 51.3 %all-to-all-start.6 = ((bf16[1024,1,5,128]{3,2,1,0:T(8,128)(2,1)}), bf16[1024,1,5,128]{3,2,1,0:T(8,128)(2,1)S(1)}, u32[]{:S(2)}, u32[]{:S(2)}) async-start(bf16[1024,1,5,128]{3,2,1,0:T(8,128)(2,1)} %bitcast.207), calls=%async_computation.6 | async-start | bytes 4194304 | tf_op jit(solution)/shard_map/all_to_all | solution.py:116
  (11 other events, 29.1 us)
Sparse Core Ops, SparseCore 0:
  85.4 240.2 all-reduce.4
  328.4 936.0 all-reduce.6
